TPU v7x, 32 devices: a whole 2x2x4 slice. The times are simulated.
32 devices in a mesh: dp: 8 (over z, y), tensor: 4 (over x, core).
Axes of the slice: x: 2, y: 2, z: 4, core: 2. Of those that a mesh axis runs over, the one named last changes fastest.
Arguments:
- hidden: bfloat16 [1536, 14336], P('dp', 'tensor'), may hold values from -0.15625 to 0.15625
- out_grad: bfloat16 [1536, 8192], P(('dp', 'tensor')), may hold values from -6 to 6
- weights: bfloat16 [4, 32, 128, 128], P('tensor'), may hold values from -0.125 to 0.125
- block_rows: int32 [4, 32], P('tensor'), may hold values from 0 to 27, as said below
- block_cols: int32 [4, 32], P('tensor'), may hold values from 0 to 63, as said below
- counts: int32 [4], P('tensor'), may hold values from 16 to 32, as said below
Outputs:
- weight_grad: float32 [4, 32, 128, 128], P('tensor', 'dp')
- input_grad: bfloat16 [1536, 14336], P('dp', 'tensor')
Inputs may be any that keep to these rules, and one draw needn't show every extreme that they name: `block_rows`: within one member, no two slots name the same pair of block row and block column. `block_cols`: pairs with block_rows as stated there. `counts`: some member has all 32 slots live.
All inputs are finite; a program needn't handle non-finite values.
Results may differ from a plain program's by a relative error of at most 0.001.
Values may be sent and summed in bfloat16 or wider, within the bound.
A program may use at most 128 MiB of HBM per device.

v0:
```python
import math

import jax
import jax.numpy as jnp
from jax import lax
from jax.sharding import PartitionSpec as P

BLK = 128


def shards(hidden, out_grad, weights, block_rows, block_cols, counts):
    slot_weights = weights[0]
    position_rows = block_rows[0]
    slot_cols = block_cols[0]
    panel_blocks = hidden.shape[1] // BLK
    col_blocks = out_grad.shape[1] // BLK
    active_flags = (jnp.arange(position_rows.shape[0], dtype=jnp.int32) < counts[0]).astype(
        jnp.float32
    )
    assignment = (
        position_rows[:, None] == jnp.arange(panel_blocks, dtype=jnp.int32)[None, :]
    ).astype(jnp.float32)
    assignment = assignment * active_flags[:, None]
    initial = (jnp.zeros(slot_weights.shape, jnp.float32), jnp.zeros(hidden.shape, jnp.float32))
    rows_piece = lax.all_gather(out_grad, "tensor", axis=0, tiled=True)
    height = rows_piece.shape[0]
    stride = math.gcd(height, 256)

    def row_step(position, sums):
        gradient_accumulator, input_acc = sums
        first_row = position * stride
        grad_rows = lax.dynamic_slice_in_dim(rows_piece, first_row, stride, 0)
        act_rows = lax.dynamic_slice_in_dim(hidden, first_row, stride, 0)
        grad_sel = jnp.take(grad_rows.reshape(stride, col_blocks, BLK), slot_cols, axis=1)
        act_sel = jnp.take(act_rows.reshape(stride, panel_blocks, BLK), position_rows, axis=1)
        gradient_accumulator = gradient_accumulator + jnp.einsum(
            "nsa,nsb->sab", act_sel, grad_sel, preferred_element_type=jnp.float32
        )
        contribution = jnp.einsum(
            "nsb,sab->nsa", grad_sel, slot_weights, preferred_element_type=jnp.float32
        )
        placed = jnp.einsum(
            "nsa,sp->npa", contribution, assignment, precision=lax.Precision.HIGHEST
        )
        input_acc = lax.dynamic_update_slice_in_dim(
            input_acc, placed.reshape(stride, -1), first_row, 0
        )
        return (gradient_accumulator, input_acc)

    gradient_accumulator, input_acc = lax.fori_loop(0, height // stride, row_step, initial)
    gradient_accumulator = gradient_accumulator * active_flags[:, None, None]
    mine = lax.psum_scatter(gradient_accumulator, "dp", scatter_dimension=0, tiled=True)
    return (mine[None], input_acc.astype(jnp.bfloat16))


def solution(mesh):
    in_specs = (
        P("dp", "tensor"),
        P(("dp", "tensor"), None),
        P("tensor", None, None, None),
        P("tensor", None),
        P("tensor", None),
        P("tensor"),
    )
    out_specs = (P("tensor", "dp", None, None), P("dp", "tensor"))
    return jax.shard_map(shards, mesh=mesh, in_specs=in_specs, out_specs=out_specs, check_vma=False)
```

profile of v0, /device:TPU:0, one launch (start us, length us, event | category | flops | bytes accessed | tf_op | source)
XLA Modules:
  0.0 154.4 jit_solution(14075374970134248380)
XLA Ops:
  7.2 0.0 copy-start.1
  7.2 0.0 copy-start
  7.2 0.0 all-gather.2.cloned.1.call-start
  7.2 0.7 all-gather.2.cloned.1.call-update
  7.9 0.0 reduce-scatter.2.cloned.1.call-start
  8.6 32.2 %all-gather.2.cloned.1.call-done = bf16[192,8192]{1,0:T(8,128)(2,1)} async-done(((bf16[48,8192]{1,0:T(8,128)(2,1)}), bf16[192,8192]{1,0:T(8,128)(2,1)}) %all-gather.2.cloned.1.call-update) | async-done | bytes 3145744 | tf_op jit(solution)/shard_map/all_gather | solution.py:25
  40.8 1.2 broadcast_in_dim.47
  42.0 0.0 copy-done.1
  42.0 0.0 copy-done
  42.0 35.9 %while.18 = (s32[]{:T(128)}, f32[32,128,128]{2,1,0:T(8,128)S(1)}, bf16[192,3584]{1,0:T(8,128)(2,1)}, s32[32]{0:T(128)S(1)}, bf16[192,3584]{1,0:T(8,128)(2,1)}, /...) while((s32[]{:T(128)}, f32[32,128,128]{2,1,0:T(8,128)S(1)}, ...), condition=%wide.region_1.0_spmd.clone.clone.clone, body=%wide.region_0.1_spmd.clone.clone.clone.sunk | while | flops 224137536 | bytes 15411049 | solution.py:50
  42.1 1.1 copy_bitcast_fusion.4
  43.2 0.6 gather_fusion
  43.9 2.5 %copy_bitcast_fusion.5 = bf16[64,64,128]{2,0,1:T(8,128)(2,1)} fusion(bf16[192,8192]{1,0:T(8,128)(2,1)} %get-tuple-element.359, s32[]{:T(128)S(6)} %select_n.125), kind=kLoop, calls=%fused_computation.5.clone.1 | loop fusion | bytes 2097156 | tf_op jit(solution)/shard_map/while/body/eval_jaxpr/reshape | solution.py:34
  46.4 1.9 %gather_fusion.1 = bf16[32,64,128]{2,1,0:T(8,128)(2,1)S(1)} fusion(bf16[64,64,128]{2,0,1:T(8,128)(2,1)} %copy_bitcast_fusion.5, s32[1024]{0:T(1024)S(1)} %pad_clamp_fusion.5), kind=kCustom, calls=%fused_computation.1.clone.clone.clone.clone.1 | custom fusion | bytes 1048704 | tf_op jit(solution)/shard_map/while/body/eval_jaxpr/jit(_take)/gather | solution.py:34
  48.3 2.1 %convolution_bitcast_fusion.2 = f32[64,32,128]{2,0,1:T(8,128)S(1)} fusion(bf16[32,128,128]{2,1,0:T(8,128)(2,1)} %get-tuple-element.360, bf16[32,64,128]{2,1,0:T(8,128)(2,1)S(1)} %gather_fusion.1, pred[32]{0:T(512)(128)(4,1)S(1)} %get-tuple-element.326), kind=kOutput, calls=%fused_computation.4.clone.1 | convolution fusion | flops 67371008 | bytes 2621472 | tf_op jit(solution)/shard_map/while/body/eval_jaxpr/nsb,sab->nsa/dot_general | solution.py:39
  50.3 1.7 %fusion.36 = bf16[64,128,28]{1,2,0:T(8,128)(2,1)S(1)} fusion(f32[64,32,128]{2,0,1:T(8,128)S(1)} %convolution_bitcast_fusion.2, f32[32]{0:T(128)S(1)} %get-tuple-element.361, s32[32]{0:T(128)S(1)} %get-tuple-element.356), kind=kOutput, calls=%fused_computation.6.clone.1 | convolution fusion | flops 88082176 | bytes 1507584 | tf_op jit(solution)/shard_map/while/body/eval_jaxpr/nsa,sp->npa/dot_general | solution.py:42
  52.0 0.9 bitcast_dynamic-update-slice_fusion.2
  52.9 1.0 select_add_fusion.2
  54.0 1.1 copy_bitcast_fusion.4
  55.2 0.6 gather_fusion
  55.8 2.5 %copy_bitcast_fusion.5 = bf16[64,64,128]{2,0,1:T(8,128)(2,1)} fusion(bf16[192,8192]{1,0:T(8,128)(2,1)} %get-tuple-element.359, s32[]{:T(128)S(6)} %select_n.125), kind=kLoop, calls=%fused_computation.5.clone.1 | loop fusion | bytes 2097156 | tf_op jit(solution)/shard_map/while/body/eval_jaxpr/reshape | solution.py:34
  58.3 1.9 %gather_fusion.1 = bf16[32,64,128]{2,1,0:T(8,128)(2,1)S(1)} fusion(bf16[64,64,128]{2,0,1:T(8,128)(2,1)} %copy_bitcast_fusion.5, s32[1024]{0:T(1024)S(1)} %pad_clamp_fusion.5), kind=kCustom, calls=%fused_computation.1.clone.clone.clone.clone.1 | custom fusion | bytes 1048704 | tf_op jit(solution)/shard_map/while/body/eval_jaxpr/jit(_take)/gather | solution.py:34
  60.2 2.1 %convolution_bitcast_fusion.2 = f32[64,32,128]{2,0,1:T(8,128)S(1)} fusion(bf16[32,128,128]{2,1,0:T(8,128)(2,1)} %get-tuple-element.360, bf16[32,64,128]{2,1,0:T(8,128)(2,1)S(1)} %gather_fusion.1, pred[32]{0:T(512)(128)(4,1)S(1)} %get-tuple-element.326), kind=kOutput, calls=%fused_computation.4.clone.1 | convolution fusion | flops 67371008 | bytes 2621472 | tf_op jit(solution)/shard_map/while/body/eval_jaxpr/nsb,sab->nsa/dot_general | solution.py:39
  62.3 1.7 %fusion.36 = bf16[64,128,28]{1,2,0:T(8,128)(2,1)S(1)} fusion(f32[64,32,128]{2,0,1:T(8,128)S(1)} %convolution_bitcast_fusion.2, f32[32]{0:T(128)S(1)} %get-tuple-element.361, s32[32]{0:T(128)S(1)} %get-tuple-element.356), kind=kOutput, calls=%fused_computation.6.clone.1 | convolution fusion | flops 88082176 | bytes 1507584 | tf_op jit(solution)/shard_map/while/body/eval_jaxpr/nsa,sp->npa/dot_general | solution.py:42
  64.0 0.9 bitcast_dynamic-update-slice_fusion.2
  64.9 1.0 select_add_fusion.2
  66.0 1.1 copy_bitcast_fusion.4
  67.2 0.6 gather_fusion
  67.8 2.5 %copy_bitcast_fusion.5 = bf16[64,64,128]{2,0,1:T(8,128)(2,1)} fusion(bf16[192,8192]{1,0:T(8,128)(2,1)} %get-tuple-element.359, s32[]{:T(128)S(6)} %select_n.125), kind=kLoop, calls=%fused_computation.5.clone.1 | loop fusion | bytes 2097156 | tf_op jit(solution)/shard_map/while/body/eval_jaxpr/reshape | solution.py:34
  70.3 1.9 %gather_fusion.1 = bf16[32,64,128]{2,1,0:T(8,128)(2,1)S(1)} fusion(bf16[64,64,128]{2,0,1:T(8,128)(2,1)} %copy_bitcast_fusion.5, s32[1024]{0:T(1024)S(1)} %pad_clamp_fusion.5), kind=kCustom, calls=%fused_computation.1.clone.clone.clone.clone.1 | custom fusion | bytes 1048704 | tf_op jit(solution)/shard_map/while/body/eval_jaxpr/jit(_take)/gather | solution.py:34
  72.2 2.1 %convolution_bitcast_fusion.2 = f32[64,32,128]{2,0,1:T(8,128)S(1)} fusion(bf16[32,128,128]{2,1,0:T(8,128)(2,1)} %get-tuple-element.360, bf16[32,64,128]{2,1,0:T(8,128)(2,1)S(1)} %gather_fusion.1, pred[32]{0:T(512)(128)(4,1)S(1)} %get-tuple-element.326), kind=kOutput, calls=%fused_computation.4.clone.1 | convolution fusion | flops 67371008 | bytes 2621472 | tf_op jit(solution)/shard_map/while/body/eval_jaxpr/nsb,sab->nsa/dot_general | solution.py:39
  74.3 1.7 %fusion.36 = bf16[64,128,28]{1,2,0:T(8,128)(2,1)S(1)} fusion(f32[64,32,128]{2,0,1:T(8,128)S(1)} %convolution_bitcast_fusion.2, f32[32]{0:T(128)S(1)} %get-tuple-element.361, s32[32]{0:T(128)S(1)} %get-tuple-element.356), kind=kOutput, calls=%fused_computation.6.clone.1 | convolution fusion | flops 88082176 | bytes 1507584 | tf_op jit(solution)/shard_map/while/body/eval_jaxpr/nsa,sp->npa/dot_general | solution.py:42
  76.0 0.9 bitcast_dynamic-update-slice_fusion.2
  76.9 1.0 select_add_fusion.2
  77.9 1.6 %broadcast_multiply_fusion = f32[32,128,128]{2,1,0:T(8,128)} fusion(f32[32,128,128]{2,1,0:T(8,128)S(1)} %get-tuple-element.157, f32[32]{0:T(128)S(1)} %get-tuple-element.373), kind=kLoop, calls=%fused_computation.38 | loop fusion | flops 524288 | bytes 4194432 | tf_op jit(solution)/shard_map/mul | solution.py:51
  79.5 0.0 reduce-scatter.2.cloned.1.call-update
  79.5 68.1 %reduce-scatter.2.cloned.1.call-done = f32[4,128,128]{2,1,0:T(8,128)} async-done(((f32[32,128,128]{2,1,0:T(8,128)}), f32[4,128,128]{2,1,0:T(8,128)}) %reduce-scatter.2.cloned.1.call-update) | async-done | bytes 262160 | tf_op jit(solution)/shard_map/reduce_scatter | solution.py:52
  (14 shorter events, 0.1 us)
Async XLA Ops:
  7.2 34.8 %copy-start.1 = (s32[1,32]{1,0:T(1,128)S(1)}, s32[1,32]{1,0:T(1,128)}, u32[]{:S(2)}) copy-start(s32[1,32]{1,0:T(1,128)} %param.12) | copy-start | bytes 388
  7.2 34.8 %copy-start = (s32[1,32]{1,0:T(1,128)S(1)}, s32[1,32]{1,0:T(1,128)}, u32[]{:S(2)}) copy-start(s32[1,32]{1,0:T(1,128)} %param.11) | copy-start | bytes 388
  7.2 33.7 %all-gather.2.cloned.1.call-start = ((), (), s32[]{:S(2)}) async-start(), calls=%async_computation.1 | async-start | bytes 3932160 | tf_op jit(solution)/shard_map/all_gather | solution.py:25
  7.9 139.7 %reduce-scatter.2.cloned.1.call-start = ((), (), s32[]{:S(2)}) async-start(), calls=%async_computation.2 | async-start | bytes 2359296 | tf_op jit(solution)/shard_map/reduce_scatter | solution.py:52
Sparse Core Ops, SparseCore 0:
  9.6 31.2 all-gather.1
  79.6 67.9 reduce-scatter.1
where the time goes:
time: 155 us; the launch traced here: 154 us
  waiting for transfers between devices  101 us (65%)
  local copies, waits for them, and re-layouts  22.5 us (15%)
  between operations  14.7 us (9%)
  matrix products  14.3 us (9%)
  other arithmetic  1.63 us (1%)
    reduce_scatter x1, waiting for transfers between devices, shards(): lax.psum_scatter(gradient_accumulator, 'dp', scatter_dimension=0, tiled=T...  68.1 us
    all_gather x1, waiting for transfers between devices, shards(): rows_piece = lax.all_gather(out_grad, 'tensor', axis=0, tiled=True)  32.2 us
    reshape x3, local copies, waits for them, and re-layouts, row_step(): grad_rows.reshape(stride, col_blocks, BLK)  7.53 us
    dot_general x3, matrix products, row_step(): jnp.einsum('nsb,sab->nsa', grad_sel, slot_weights, preferred_element_type...  6.2 us
    gather x3, local copies, waits for them, and re-layouts, row_step(): jnp.take(grad_rows.reshape(stride, col_blocks, BLK), slot_cols, axis=1)  5.61 us
    dot_general x3, matrix products, row_step(): jnp.einsum('nsa,sp->npa', contribution, assignment, precision=lax.Precisi...  5.05 us
    reshape x3, local copies, waits for them, and re-layouts, row_step(): act_rows.reshape(stride, panel_blocks, BLK)  3.42 us
  transfers between devices with their start and end apart: 2, of which 2 were waited for; matrix products, arithmetic and copies ran while one was open for 0% of the time, Pallas kernels for 0%

commit v1 on v0

v1 whole, which is shorter than its diff:
```python
import functools

import jax
import jax.numpy as jnp
from jax import lax
from jax.experimental import pallas as pl
from jax.experimental.pallas import tpu as pltpu
from jax.sharding import PartitionSpec as P

MESH = pl.DeviceIdType.MESH


def kernel(
    n_t,
    n_dp,
    per,
    panel,
    meta,
    cols_ref,
    hid_hbm,
    og_hbm,
    w_hbm,
    wg_out,
    ig_out,
    hid,
    og,
    w,
    allcols,
    cols_sm,
    sbuf,
    gbuf,
    part,
    recv,
    runs,
    ig,
    in_sem,
    sm_sem,
    c_send,
    c_recv,
    g_send,
    g_recv,
    r_send,
    r_recv,
    out_sem,
):
    slots = per * n_dp
    rows = og.shape[1]
    blk = w.shape[1]
    stages = n_dp.bit_length() - 1
    me_t = lax.axis_index("tensor")
    me_d = lax.axis_index("dp")

    w_in = pltpu.make_async_copy(w_hbm, w, in_sem.at[2])

    def load(src, dst, sem):
        def one(c, carry):
            columns = pl.ds(pl.multiple_of(c * blk, blk), blk)
            pltpu.make_async_copy(src.at[:, columns], dst.at[c], sem).start()
            return carry

        lax.fori_loop(0, dst.shape[0], one, 0)

    load(og_hbm, og, in_sem.at[0])

    def peer(r):
        return lax.rem(me_t + r, n_t)

    def source(r):
        return lax.rem(me_t + n_t - r, n_t)

    def bit(b):
        return lax.rem(me_d // (1 << b), 2)

    def partner(b):
        return me_d + (1 << b) * (1 - 2 * bit(b))

    barrier = pltpu.get_barrier_semaphore()
    for r in range(1, n_t):
        pl.semaphore_signal(barrier, inc=1, device_id={"tensor": peer(r)}, device_id_type=MESH)
    for b in range(stages):
        pl.semaphore_signal(barrier, inc=1, device_id={"dp": partner(b)}, device_id_type=MESH)
    pl.semaphore_wait(barrier, n_t - 1 + stages)

    col_copies = []
    for r in range(1, n_t):
        copy = pltpu.make_async_remote_copy(
            src_ref=cols_ref,
            dst_ref=allcols.at[r],
            send_sem=c_send.at[r],
            recv_sem=c_recv.at[r],
            device_id={"tensor": peer(r)},
            device_id_type=MESH,
        )
        copy.start()
        col_copies.append(copy)
    own_cols = pltpu.make_async_copy(cols_ref, cols_sm.at[0], sm_sem.at[0])
    own_cols.start()
    load(hid_hbm, hid, in_sem.at[1])
    w_in.start()
    runs[slots] = jnp.zeros(runs.shape[1:], jnp.float32)
    for r in range(1, n_t):
        col_copies[r - 1].wait_recv()
        pltpu.make_async_copy(allcols.at[r], cols_sm.at[r], sm_sem.at[r]).start()
    for r in range(1, n_t):
        pltpu.make_async_copy(allcols.at[r], cols_sm.at[r], sm_sem.at[r]).wait()
    own_cols.wait()
    pltpu.make_async_copy(og, og, in_sem.at[0]).wait()

    def gather_copy(r, j):
        return pltpu.make_async_remote_copy(
            src_ref=sbuf.at[r, pl.ds(j * n_dp, n_dp)],
            dst_ref=gbuf.at[pl.ds(j * n_dp, n_dp), pl.ds(pl.multiple_of(me_t * rows, 16), rows)],
            send_sem=g_send.at[r, j],
            recv_sem=g_recv.at[r, j],
            device_id={"tensor": peer(r)},
            device_id_type=MESH,
        )

    def block_of(r, k):
        return og[cols_sm[r, 0, k]]

    order = sorted(range(1, n_t), key=lambda r: -min(r, n_t - r))
    for j in range(per):
        for r in order:

            def pick(q, carry, r=r, j=j):
                sbuf[r, j * n_dp + q] = block_of(n_t - r, j * n_dp + q)
                return carry

            lax.fori_loop(0, n_dp, pick, 0)
            gather_copy(r, j).start()

    def own(k, carry):
        gbuf[k, pl.ds(pl.multiple_of(me_t * rows, 16), rows)] = block_of(0, k)
        return carry

    lax.fori_loop(0, slots, own, 0)
    pltpu.make_async_copy(hid, hid, in_sem.at[1]).wait()
    w_in.wait()

    def base(level):
        first = 0
        for b in range(level):
            first = first + bit(b) * (n_dp >> (b + 1))
        return first

    def offset(b):
        return sum(n_dp >> (i + 1) for i in range(b))

    def reduce_copy(j, b):
        half = n_dp >> (b + 1)
        return pltpu.make_async_remote_copy(
            src_ref=part.at[j, pl.ds(base(b) + (1 - bit(b)) * half, half)],
            dst_ref=recv.at[j, pl.ds(offset(b), half)],
            send_sem=r_send.at[j, b],
            recv_sem=r_recv.at[j, b],
            device_id={"dp": partner(b)},
            device_id_type=MESH,
        )

    def slot_of(j, q):
        d = 0
        for b in range(stages):
            d = d + lax.rem(q // (1 << b), 2) * (n_dp >> (b + 1))
        return d * per + j

    def products(j, first, count):
        def one(i, carry):
            q = first + i
            k = j * n_dp + q
            h = hid[meta[k]]
            part[j, q] = lax.dot_general(
                h, gbuf[k], (((0,), (0,)), ((), ())), preferred_element_type=jnp.float32
            )
            return carry

        lax.fori_loop(0, count, one, 0)

    def contributions(j):
        def one(q, carry):
            k = j * n_dp + q
            c = lax.dot_general(
                gbuf[k], w[slot_of(j, q)], (((1,), (1,)), ((), ())), preferred_element_type=jnp.float32
            )
            runs[k] = c + runs[meta[slots + k]]
            return carry

        lax.fori_loop(0, n_dp, one, 0)

    def first_half(j):
        for r in range(1, n_t):
            gather_copy(r, j).wait_recv()
        half = n_dp // 2
        products(j, (1 - bit(0)) * half, half)
        reduce_copy(j, 0).start()
        products(j, bit(0) * half, half)
        contributions(j)

    def advance(j, b):
        half = n_dp >> (b + 1)
        reduce_copy(j, b).wait_recv()
        mine = base(b + 1)

        def add(i, carry):
            part[j, mine + i] = part[j, mine + i] + recv[j, offset(b) + i]
            return carry

        lax.fori_loop(0, half, add, 0)
        if b + 1 < stages:
            reduce_copy(j, b + 1).start()

    def write_out():
        for p in range(panel):
            ig[:, p * blk : (p + 1) * blk] = runs[meta[2 * slots + p]].astype(ig.dtype)

    ig_copy = pltpu.make_async_copy(ig, ig_out, out_sem.at[0])
    for step in range(per + stages):
        if step < per:
            first_half(step)
        if step == per - 1:
            write_out()
            ig_copy.start()
        for b in reversed(range(stages)):
            j = step - 1 - b
            if 0 <= j < per:
                advance(j, b)
    wg_copies = []
    for j in range(per):
        copy = pltpu.make_async_copy(part.at[j, base(stages)], wg_out.at[j], out_sem.at[1 + j])
        copy.start()
        wg_copies.append(copy)
    for r in range(1, n_t):
        col_copies[r - 1].wait_send()
        for j in range(per):
            gather_copy(r, j).wait_send()
    for j in range(per):
        for b in range(stages):
            reduce_copy(j, b).wait_send()
        wg_copies[j].wait()
    ig_copy.wait()


def shards(n_t, n_dp, hidden, out_grad, weights, block_rows, block_cols, counts):
    w = weights[0]
    slots, blk, _ = w.shape
    tokens, width = hidden.shape
    rows = out_grad.shape[0]
    panel = width // blk
    per = slots // n_dp
    stages = n_dp.bit_length() - 1

    def arranged(a):
        return a.reshape((2,) * stages + (per,)).transpose(*reversed(range(stages + 1))).reshape(slots)

    rows_k = arranged(block_rows[0])
    cols_k = arranged(block_cols[0])
    live_k = arranged(jnp.arange(slots, dtype=jnp.int32)) < counts[0]
    index = jnp.arange(slots, dtype=jnp.int32)
    wanted = jnp.concatenate([rows_k, jnp.arange(panel, dtype=jnp.int32)])
    limit = jnp.concatenate([index, jnp.full((panel,), slots, jnp.int32)])
    match = (wanted[:, None] == rows_k[None, :]) & live_k[None, :] & (index[None, :] < limit[:, None])
    found = jnp.max(jnp.where(match, index[None, :], -1), axis=1)
    meta = jnp.concatenate([rows_k, jnp.where(found < 0, slots, found)])
    cols = jnp.pad(cols_k[None, :], ((0, 0), (0, 128 - slots)))

    anyspace = pl.BlockSpec(memory_space=pl.ANY)
    flops = 4 * slots * tokens * blk * blk
    wg, ig = pl.pallas_call(
        functools.partial(kernel, n_t, n_dp, per, panel),
        out_shape=(
            jax.ShapeDtypeStruct((per, blk, blk), jnp.float32),
            jax.ShapeDtypeStruct((tokens, width), jnp.bfloat16),
        ),
        in_specs=[
            pl.BlockSpec(memory_space=pltpu.SMEM),
            pl.BlockSpec(memory_space=pltpu.VMEM),
            anyspace,
            anyspace,
            anyspace,
        ],
        out_specs=(anyspace, anyspace),
        scratch_shapes=[
            pltpu.VMEM((panel, tokens, blk), jnp.bfloat16),
            pltpu.VMEM((out_grad.shape[1] // blk, rows, blk), jnp.bfloat16),
            pltpu.VMEM(w.shape, jnp.bfloat16),
            pltpu.VMEM((n_t, 1, 128), jnp.int32),
            pltpu.SMEM((n_t, 1, 128), jnp.int32),
            pltpu.VMEM((n_t, slots, rows, blk), jnp.bfloat16),
            pltpu.VMEM((slots, tokens, blk), jnp.bfloat16),
            pltpu.VMEM((per, n_dp, blk, blk), jnp.float32),
            pltpu.VMEM((per, n_dp, blk, blk), jnp.float32),
            pltpu.VMEM((slots + 1, tokens, blk), jnp.float32),
            pltpu.VMEM((tokens, width), jnp.bfloat16),
            pltpu.SemaphoreType.DMA((3,)),
            pltpu.SemaphoreType.DMA((n_t,)),
            pltpu.SemaphoreType.DMA((n_t,)),
            pltpu.SemaphoreType.DMA((n_t,)),
            pltpu.SemaphoreType.DMA((n_t, per)),
            pltpu.SemaphoreType.DMA((n_t, per)),
            pltpu.SemaphoreType.DMA((per, stages)),
            pltpu.SemaphoreType.DMA((per, stages)),
            pltpu.SemaphoreType.DMA((1 + per,)),
        ],
        compiler_params=pltpu.CompilerParams(
            collective_id=0, has_side_effects=True, vmem_limit_bytes=52 * 2**20
        ),
        cost_estimate=pl.CostEstimate(flops=flops, bytes_accessed=6 * 2**20, transcendentals=0),
    )(meta, cols, hidden, out_grad, w)
    live = lax.axis_index("dp") * per + jnp.arange(per, dtype=jnp.int32) < counts[0]
    return jnp.where(live[:, None, None], wg, 0.0)[None], ig


def solution(mesh):
    in_specs = (
        P("dp", "tensor"),
        P(("dp", "tensor"), None),
        P("tensor", None, None, None),
        P("tensor", None),
        P("tensor", None),
        P("tensor"),
    )
    out_specs = (P("tensor", "dp", None, None), P("dp", "tensor"))
    body = functools.partial(shards, mesh.shape["tensor"], mesh.shape["dp"])
    return jax.shard_map(body, mesh=mesh, in_specs=in_specs, out_specs=out_specs, check_vma=False)
```

time: 155 us -> 63 us (0.41)
  waiting for transfers between devices: 101 us -> 0 us
  Pallas kernels: 0 us -> 52.2 us
  local copies, waits for them, and re-layouts: 22.5 us -> 4.85 us
  matrix products: 14.3 us -> 0 us
  between operations: 14.7 us -> 1.33 us
  other arithmetic: 1.63 us -> 4.36 us
    reduce_scatter x1 -> x0, waiting for transfers between devices: 68.1 us -> none  [shards(): lax.psum_scatter(gradient_accumulator, 'dp', scatter_dimension=0, tiled=T...]
    pallas_call x0 -> x1, Pallas kernels: none -> 52.2 us  [shards(): pl.pallas_call(functools.partial(kernel, n_t, n_dp, per, panel), out_shap...]
    all_gather x1 -> x0, waiting for transfers between devices: 32.2 us -> none  [shards(): rows_piece = lax.all_gather(out_grad, 'tensor', axis=0, tiled=True)]
    dot_general x9 -> x0, matrix products: 14.3 us -> none  [the longest x3 6.2 us: row_step(): jnp.einsum('nsb,sab->nsa', grad_sel, slot_weights, preferred_element_type...]
    reshape x6 -> x1, local copies, waits for them, and re-layouts: 10.9 us -> 0.1 us  [arranged(): a.reshape((2,) * stages + (per,)).transpose(*reversed(range(stages + 1)))]
    gather x6 -> x0, local copies, waits for them, and re-layouts: 7.56 us -> none  [the longest x3 5.61 us: row_step(): jnp.take(grad_rows.reshape(stride, col_blocks, BLK), slot_cols, axis=1)]
    unnamed x4, local copies, waits for them, and re-layouts: 0.01 us -> 4.15 us
    dynamic_update_slice x3 -> x0, local copies, waits for them, and re-layouts: 2.77 us -> none  [row_step(): lax.dynamic_update_slice_in_dim(input_acc, placed.reshape(stride, -1), fi...]
  transfers between devices with their start and end apart: 2 -> 0, of which waited for: 2 -> 0; matrix products, arithmetic and copies ran while one was open for 0% -> 0% of each run, Pallas kernels for 0% -> 0%
where the time goes in v1:
time: 63 us; the launch traced here: 62.8 us
  Pallas kernels  52.2 us (83%)
  local copies, waits for them, and re-layouts  4.85 us (8%)
  other arithmetic  4.36 us (7%)
  between operations  1.33 us (2%)
    pallas_call x1, Pallas kernels, shards(): pl.pallas_call(functools.partial(kernel, n_t, n_dp, per, panel), out_shap...  52.2 us
    unnamed x4, local copies, waits for them, and re-layouts  4.15 us
    unnamed x2, other arithmetic  2.64 us

profile of v1, /device:TPU:0, one launch (start us, length us, event | category | flops | bytes accessed | tf_op | source)
XLA Modules:
  0.0 62.8 jit_solution(9280103082589888324)
XLA Ops:
  1.3 0.5 broadcast.61
  1.8 1.3 %reduce.6 = s32[32]{0:T(128)S(1)} reduce(s32[1,32]{1,0:T(1,128)} %param.9, s32[]{:T(128)} %broadcast.61), dimensions={0}, to_apply=%param.9.reduce_sub_computation.3 | reduce | bytes 260 | tf_op args[3]
  3.1 1.3 %reduce.7 = s32[32]{0:T(128)S(1)} reduce(s32[1,32]{1,0:T(1,128)} %param.10, s32[]{:T(128)} %broadcast.61), dimensions={0}, to_apply=%param.10.reduce_sub_computation.3 | reduce | bytes 260 | tf_op args[4]
  4.4 0.1 reshape_squeeze.7
  4.5 0.1 reshape_squeeze.6
  4.6 0.1 copy.12
  4.7 0.1 reshape.73
  4.8 0.1 pad_add_fusion
  4.9 0.1 copy.13
  5.0 0.1 broadcast_in_dim_reshape.4
  5.2 0.1 reshape.85
  5.3 0.8 %select_reduce_fusion = s32[60]{0:T(128)S(1)} fusion(s32[60]{0:T(128)} %constant.21.clone.1, s32[60]{0:T(128)S(1)} %pad_add_fusion, s32[32]{0:T(128)S(1)} %reshape.73, pred[32]{0:T(512)(128)(4,1)S(1)} %reshape.85), kind=kLoop, calls=%fused_computation.1 | loop fusion | flops 11460 | bytes 880 | tf_op jit(solution)/shard_map/reduce_max | solution.py:262
  6.0 0.1 pad_add_fusion.1.meta
  6.1 0.0 copy-start
  6.1 1.1 %copy-done = bf16[48,8192]{1,0:T(8,128)(2,1)S(1)} copy-done((bf16[48,8192]{1,0:T(8,128)(2,1)S(1)}, bf16[48,8192]{1,0:T(8,128)(2,1)}, u32[]{:S(2)}) %copy-start) | copy-done | bytes 786456
  7.2 52.2 %shard_map.77 = (f32[4,128,128]{2,1,0:T(8,128)S(1)}, bf16[192,3584]{1,0:T(8,128)(2,1)}) custom-call(s32[92]{0:T(128)S(1)} %pad_add_fusion.1.meta, s32[1,128]{1,0:T(1,128)S(1)} %pad.5.cols_ref, bf16[192,3584]{1,0:T(8,128)(2,1)} %hid_hbm.1, bf16[48,8192]{1,0:T(8,128)(2,1)S(1)} %copy-done, bf16[32,128,128]{2,1,0:T(8,128)(2,1)} %bitcast.8), custom_call_target="tpu_custom_call" | custom-call | flops 402653184 | bytes 6291456 | tf_op jit(solution)/shard_map/pallas_call | solution.py:268
  59.5 0.8 %select_bitcast_fusion = f32[1,4,128,128]{3,2,1,0:T(8,128)} fusion(f32[4,128,128]{2,1,0:T(8,128)S(1)} %get-tuple-element.4, pred[4]{0:T(512)(128)(4,1)S(1)} %add_compare_fusion.1), kind=kLoop, calls=%fused_computation | loop fusion | flops 65536 | bytes 524292 | tf_op jit(solution)/shard_map/broadcast_in_dim | solution.py:310
  60.3 2.5 %copy.16 = bf16[192,3584]{1,0:T(8,128)(2,1)} copy(bf16[192,3584]{1,0:T(8,128)(2,1)} %get-tuple-element.9) | data formatting | bytes 2752512
  (5 shorter events, 0.0 us)
Async XLA Ops:
  6.1 1.1 %copy-start = (bf16[48,8192]{1,0:T(8,128)(2,1)S(1)}, bf16[48,8192]{1,0:T(8,128)(2,1)}, u32[]{:S(2)}) copy-start(bf16[48,8192]{1,0:T(8,128)(2,1)} %og_hbm.1) | copy-start | bytes 2359300

commit v2 on v1

--- a/solution.py
+++ b/solution.py
@@ -15,7 +15,8 @@
     n_dp,
     per,
     panel,
-    meta,
+    counts,
+    rows_ref,
     cols_ref,
     hid_hbm,
     og_hbm,
@@ -27,6 +28,9 @@
     w,
     allcols,
     cols_sm,
+    key,
+    before,
+    last,
     sbuf,
     gbuf,
     part,
@@ -71,6 +75,18 @@
     def bit(b):
         return lax.rem(me_d // (1 << b), 2)
 
+    def bits(j):
+        listed = list(range(stages))
+        if j % 4 == 1 and stages > 1:
+            listed[:2] = [1, 0]
+        return listed
+
+    def slot_of(j, q):
+        d = 0
+        for level, b in enumerate(bits(j)):
+            d = d + lax.rem(q // (n_dp >> (level + 1)), 2) * (1 << b)
+        return d * per + j
+
     def partner(b):
         return me_d + (1 << b) * (1 - 2 * bit(b))
 
@@ -116,65 +132,88 @@
             device_id_type=MESH,
         )
 
-    def block_of(r, k):
-        return og[cols_sm[r, 0, k]]
+    def block_of(r, j, q):
+        return og[cols_sm[r, 0, slot_of(j, q)]]
 
     order = sorted(range(1, n_t), key=lambda r: -min(r, n_t - r))
     for j in range(per):
         for r in order:
 
             def pick(q, carry, r=r, j=j):
-                sbuf[r, j * n_dp + q] = block_of(n_t - r, j * n_dp + q)
+                sbuf[r, j * n_dp + q] = block_of(n_t - r, j, q)
                 return carry
 
-            lax.fori_loop(0, n_dp, pick, 0)
+            lax.fori_loop(0, n_dp, pick, 0, unroll=min(n_dp, 8))
             gather_copy(r, j).start()
 
-    def own(k, carry):
-        gbuf[k, pl.ds(pl.multiple_of(me_t * rows, 16), rows)] = block_of(0, k)
+    for j in range(per):
+
+        def own(q, carry, j=j):
+            gbuf[j * n_dp + q, pl.ds(pl.multiple_of(me_t * rows, 16), rows)] = block_of(0, j, q)
+            return carry
+
+        lax.fori_loop(0, n_dp, own, 0, unroll=min(n_dp, 8))
+
+    for j in range(per):
+
+        def mark(q, carry, j=j):
+            slot = slot_of(j, q)
+            key[j * n_dp + q] = jnp.where(slot < counts[0], rows_ref[0, slot], -1)
+            return carry
+
+        lax.fori_loop(0, n_dp, mark, 0, unroll=min(n_dp, 8))
+
+    def find_before(k, carry):
+        found = slots
+        for k2 in range(slots):
+            found = jnp.where((key[k2] == key[k]) & (k2 < k), k2, found)
+        before[k] = found
         return carry
 
-    lax.fori_loop(0, slots, own, 0)
+    lax.fori_loop(0, slots, find_before, 0)
+
+    def find_last(p, carry):
+        found = slots
+        for k2 in range(slots):
+            found = jnp.where(key[k2] == p, k2, found)
+        last[p] = found
+        return carry
+
+    lax.fori_loop(0, panel, find_last, 0)
     pltpu.make_async_copy(hid, hid, in_sem.at[1]).wait()
     w_in.wait()
 
-    def base(level):
+    def base(j, level):
         first = 0
-        for b in range(level):
-            first = first + bit(b) * (n_dp >> (b + 1))
+        for i, b in enumerate(bits(j)[:level]):
+            first = first + bit(b) * (n_dp >> (i + 1))
         return first
 
     def offset(b):
         return sum(n_dp >> (i + 1) for i in range(b))
 
-    def reduce_copy(j, b):
-        half = n_dp >> (b + 1)
+    def reduce_copy(j, level):
+        half = n_dp >> (level + 1)
+        b = bits(j)[level]
         return pltpu.make_async_remote_copy(
-            src_ref=part.at[j, pl.ds(base(b) + (1 - bit(b)) * half, half)],
-            dst_ref=recv.at[j, pl.ds(offset(b), half)],
-            send_sem=r_send.at[j, b],
-            recv_sem=r_recv.at[j, b],
+            src_ref=part.at[j, pl.ds(base(j, level) + (1 - bit(b)) * half, half)],
+            dst_ref=recv.at[j, pl.ds(offset(level), half)],
+            send_sem=r_send.at[j, level],
+            recv_sem=r_recv.at[j, level],
             device_id={"dp": partner(b)},
             device_id_type=MESH,
         )
 
-    def slot_of(j, q):
-        d = 0
-        for b in range(stages):
-            d = d + lax.rem(q // (1 << b), 2) * (n_dp >> (b + 1))
-        return d * per + j
-
     def products(j, first, count):
         def one(i, carry):
             q = first + i
-            k = j * n_dp + q
-            h = hid[meta[k]]
+            h = hid[rows_ref[0, slot_of(j, q)]]
             part[j, q] = lax.dot_general(
-                h, gbuf[k], (((0,), (0,)), ((), ())), preferred_element_type=jnp.float32
+                h, gbuf[j * n_dp + q], (((0,), (0,)), ((), ())), preferred_element_type=jnp.float32
             )
             return carry
 
-        lax.fori_loop(0, count, one, 0)
+        lax.fori_loop(0, count, one, 0, unroll=min(count, 4))
 
     def contributions(j):
         def one(q, carry):
@@ -182,51 +221,56 @@
             c = lax.dot_general(
                 gbuf[k], w[slot_of(j, q)], (((1,), (1,)), ((), ())), preferred_element_type=jnp.float32
             )
-            runs[k] = c + runs[meta[slots + k]]
-            return carry
-
-        lax.fori_loop(0, n_dp, one, 0)
+            runs[k] = c + runs[before[k]]
+            return carry
+
+        lax.fori_loop(0, n_dp, one, 0, unroll=min(n_dp, 4))
 
     def first_half(j):
         for r in range(1, n_t):
             gather_copy(r, j).wait_recv()
         half = n_dp // 2
-        products(j, (1 - bit(0)) * half, half)
+        mine = bit(bits(j)[0]) * half
+        products(j, half - mine, half)
         reduce_copy(j, 0).start()
-        products(j, bit(0) * half, half)
-        contributions(j)
-
-    def advance(j, b):
-        half = n_dp >> (b + 1)
-        reduce_copy(j, b).wait_recv()
-        mine = base(b + 1)
+        products(j, mine, half)
+
+    def advance(j, level):
+        half = n_dp >> (level + 1)
+        reduce_copy(j, level).wait_recv()
+        mine = base(j, level + 1)
 
         def add(i, carry):
-            part[j, mine + i] = part[j, mine + i] + recv[j, offset(b) + i]
+            part[j, mine + i] = part[j, mine + i] + recv[j, offset(level) + i]
             return carry
 
         lax.fori_loop(0, half, add, 0)
-        if b + 1 < stages:
-            reduce_copy(j, b + 1).start()
+        if level + 1 < stages:
+            reduce_copy(j, level + 1).start()
 
     def write_out():
         for p in range(panel):
-            ig[:, p * blk : (p + 1) * blk] = runs[meta[2 * slots + p]].astype(ig.dtype)
+            ig[:, p * blk : (p + 1) * blk] = runs[last[p]].astype(ig.dtype)
 
     ig_copy = pltpu.make_async_copy(ig, ig_out, out_sem.at[0])
     for step in range(per + stages):
         if step < per:
             first_half(step)
         if step == per - 1:
+            for j in range(per // 2):
+                contributions(j)
+        for level in reversed(range(stages)):
+            j = step - 1 - level
+            if 0 <= j < per:
+                advance(j, level)
+        if step == per - 1:
+            for j in range(per // 2, per):
+                contributions(j)
             write_out()
             ig_copy.start()
-        for b in reversed(range(stages)):
-            j = step - 1 - b
-            if 0 <= j < per:
-                advance(j, b)
     wg_copies = []
     for j in range(per):
-        copy = pltpu.make_async_copy(part.at[j, base(stages)], wg_out.at[j], out_sem.at[1 + j])
+        copy = pltpu.make_async_copy(part.at[j, base(j, stages)], wg_out.at[j], out_sem.at[1 + j])
         copy.start()
         wg_copies.append(copy)
     for r in range(1, n_t):
@@ -248,22 +292,8 @@
     panel = width // blk
     per = slots // n_dp
     stages = n_dp.bit_length() - 1
-
-    def arranged(a):
-        return a.reshape((2,) * stages + (per,)).transpose(*reversed(range(stages + 1))).reshape(slots)
-
-    rows_k = arranged(block_rows[0])
-    cols_k = arranged(block_cols[0])
-    live_k = arranged(jnp.arange(slots, dtype=jnp.int32)) < counts[0]
-    index = jnp.arange(slots, dtype=jnp.int32)
-    wanted = jnp.concatenate([rows_k, jnp.arange(panel, dtype=jnp.int32)])
-    limit = jnp.concatenate([index, jnp.full((panel,), slots, jnp.int32)])
-    match = (wanted[:, None] == rows_k[None, :]) & live_k[None, :] & (index[None, :] < limit[:, None])
-    found = jnp.max(jnp.where(match, index[None, :], -1), axis=1)
-    meta = jnp.concatenate([rows_k, jnp.where(found < 0, slots, found)])
-    cols = jnp.pad(cols_k[None, :], ((0, 0), (0, 128 - slots)))
-
     anyspace = pl.BlockSpec(memory_space=pl.ANY)
+    hbm = pl.BlockSpec(memory_space=pltpu.HBM)
     flops = 4 * slots * tokens * blk * blk
     wg, ig = pl.pallas_call(
         functools.partial(kernel, n_t, n_dp, per, panel),
@@ -273,18 +303,22 @@
         ),
         in_specs=[
             pl.BlockSpec(memory_space=pltpu.SMEM),
+            pl.BlockSpec(memory_space=pltpu.SMEM),
             pl.BlockSpec(memory_space=pltpu.VMEM),
-            anyspace,
-            anyspace,
-            anyspace,
+            hbm,
+            hbm,
+            hbm,
         ],
         out_specs=(anyspace, anyspace),
         scratch_shapes=[
             pltpu.VMEM((panel, tokens, blk), jnp.bfloat16),
             pltpu.VMEM((out_grad.shape[1] // blk, rows, blk), jnp.bfloat16),
             pltpu.VMEM(w.shape, jnp.bfloat16),
-            pltpu.VMEM((n_t, 1, 128), jnp.int32),
-            pltpu.SMEM((n_t, 1, 128), jnp.int32),
+            pltpu.VMEM((n_t, 1, slots), jnp.int32),
+            pltpu.SMEM((n_t, 1, slots), jnp.int32),
+            pltpu.SMEM((slots,), jnp.int32),
+            pltpu.SMEM((slots,), jnp.int32),
+            pltpu.SMEM((panel,), jnp.int32),
             pltpu.VMEM((n_t, slots, rows, blk), jnp.bfloat16),
             pltpu.VMEM((slots, tokens, blk), jnp.bfloat16),
             pltpu.VMEM((per, n_dp, blk, blk), jnp.float32),
@@ -302,10 +336,10 @@
             pltpu.SemaphoreType.DMA((1 + per,)),
         ],
         compiler_params=pltpu.CompilerParams(
-            collective_id=0, has_side_effects=True, vmem_limit_bytes=52 * 2**20
+            collective_id=0, has_side_effects=True, vmem_limit_bytes=64 * 2**20 - 720 * 2**10
         ),
         cost_estimate=pl.CostEstimate(flops=flops, bytes_accessed=6 * 2**20, transcendentals=0),
-    )(meta, cols, hidden, out_grad, w)
+    )(counts, block_rows, block_cols, hidden, out_grad, w)
     live = lax.axis_index("dp") * per + jnp.arange(per, dtype=jnp.int32) < counts[0]
     return jnp.where(live[:, None, None], wg, 0.0)[None], ig
 

time: 63 us -> 58.9 us (0.935)
  other arithmetic: 4.36 us -> 1.75 us
  local copies, waits for them, and re-layouts: 4.85 us -> 2.5 us
  Pallas kernels: 52.2 us -> 53.1 us
    unnamed x2 -> x0, other arithmetic: 2.64 us -> none
    unnamed x4 -> x1, local copies, waits for them, and re-layouts: 4.15 us -> 2.5 us
    broadcast_in_dim x1, other arithmetic: 0.79 us -> 1.74 us  [shards(): return (jnp.where(live[:, None, None], wg, 0.0)[None], ig)]
    pallas_call x1, Pallas kernels: 52.2 us -> 53.1 us  [shards(): pl.pallas_call(functools.partial(kernel, n_t, n_dp, per, panel), out_shap...]
    reduce_max x1 -> x0, other arithmetic: 0.75 us -> none  [shards(): found = jnp.max(jnp.where(match, index[None, :], -1), axis=1)]
where the time goes in v2:
time: 58.9 us; the launch traced here: 58.7 us
  Pallas kernels  53.1 us (90%)
  local copies, waits for them, and re-layouts  2.5 us (4%)
  other arithmetic  1.75 us (3%)
  between operations  1.29 us (2%)
    pallas_call x1, Pallas kernels, shards(): pl.pallas_call(functools.partial(kernel, n_t, n_dp, per, panel), out_shap...  53.1 us
    unnamed x1, local copies, waits for them, and re-layouts  2.5 us
    broadcast_in_dim x1, other arithmetic, shards(): return (jnp.where(live[:, None, None], wg, 0.0)[None], ig)  1.74 us

profile of v2, /device:TPU:0, one launch (start us, length us, event | category | flops | bytes accessed | tf_op | source)
XLA Modules:
  0.0 58.7 jit_solution(15594324462286956685)
XLA Ops:
  1.3 53.1 %shard_map.77 = (f32[4,128,128]{2,1,0:T(8,128)}, bf16[192,3584]{1,0:T(8,128)(2,1)}) custom-call(s32[1]{0:T(128)} %copy.9.counts, s32[1,32]{1,0:T(1,128)} %rows_ref.1, s32[1,32]{1,0:T(1,128)} %cols_ref.1, bf16[192,3584]{1,0:T(8,128)(2,1)} %hid_hbm.1, bf16[48,8192]{1,0:T(8,128)(2,1)} %og_hbm.1, bf16[32,128,128]{2,1,0:T(8,128)(2,1)} %bitcast.5), custom_call_target="tpu_custom_call" | custom-call | flops 402653184 | bytes 6291456 | tf_op jit(solution)/shard_map/pallas_call | solution.py:298
  54.4 1.7 %select_bitcast_fusion = f32[1,4,128,128]{3,2,1,0:T(8,128)} fusion(f32[4,128,128]{2,1,0:T(8,128)} %get-tuple-element.4, pred[4]{0:T(512)(128)(4,1)S(1)} %add_compare_fusion), kind=kLoop, calls=%fused_computation | loop fusion | flops 65536 | bytes 524292 | tf_op jit(solution)/shard_map/broadcast_in_dim | solution.py:344
  56.2 2.5 %copy.10 = bf16[192,3584]{1,0:T(8,128)(2,1)} copy(bf16[192,3584]{1,0:T(8,128)(2,1)} %get-tuple-element.9) | data formatting | bytes 2752512
  (1 shorter events, 0.0 us)

commit v3 on v2

--- a/solution.py
+++ b/solution.py
@@ -1,4 +1,5 @@
 import functools
+import math
 
 import jax
 import jax.numpy as jnp
@@ -62,7 +63,7 @@
             pltpu.make_async_copy(src.at[:, columns], dst.at[c], sem).start()
             return carry
 
-        lax.fori_loop(0, dst.shape[0], one, 0)
+        lax.fori_loop(0, dst.shape[0], one, 0, unroll=math.gcd(dst.shape[0], 16))
 
     load(og_hbm, og, in_sem.at[0])
 
@@ -154,32 +155,6 @@
 
         lax.fori_loop(0, n_dp, own, 0, unroll=min(n_dp, 8))
 
-    for j in range(per):
-
-        def mark(q, carry, j=j):
-            slot = slot_of(j, q)
-            key[j * n_dp + q] = jnp.where(slot < counts[0], rows_ref[0, slot], -1)
-            return carry
-
-        lax.fori_loop(0, n_dp, mark, 0, unroll=min(n_dp, 8))
-
-    def find_before(k, carry):
-        found = slots
-        for k2 in range(slots):
-            found = jnp.where((key[k2] == key[k]) & (k2 < k), k2, found)
-        before[k] = found
-        return carry
-
-    lax.fori_loop(0, slots, find_before, 0)
-
-    def find_last(p, carry):
-        found = slots
-        for k2 in range(slots):
-            found = jnp.where(key[k2] == p, k2, found)
-        last[p] = found
-        return carry
-
-    lax.fori_loop(0, panel, find_last, 0)
     pltpu.make_async_copy(hid, hid, in_sem.at[1]).wait()
     w_in.wait()
 
@@ -244,9 +219,37 @@
             part[j, mine + i] = part[j, mine + i] + recv[j, offset(level) + i]
             return carry
 
-        lax.fori_loop(0, half, add, 0)
+        lax.fori_loop(0, half, add, 0, unroll=min(half, 4))
         if level + 1 < stages:
             reduce_copy(j, level + 1).start()
+
+    def search():
+        for j in range(per):
+
+            def mark(q, carry, j=j):
+                slot = slot_of(j, q)
+                key[j * n_dp + q] = jnp.where(slot < counts[0], rows_ref[0, slot], -1)
+                return carry
+
+            lax.fori_loop(0, n_dp, mark, 0, unroll=min(n_dp, 8))
+
+        def find_before(k, carry):
+            found = slots
+            for k2 in range(slots):
+                found = jnp.where((key[k2] == key[k]) & (k2 < k), k2, found)
+            before[k] = found
+            return carry
+
+        lax.fori_loop(0, slots, find_before, 0)
+
+        def find_last(p, carry):
+            found = slots
+            for k2 in range(slots):
+                found = jnp.where(key[k2] == p, k2, found)
+            last[p] = found
+            return carry
+
+        lax.fori_loop(0, panel, find_last, 0)
 
     def write_out():
         for p in range(panel):
@@ -256,6 +259,8 @@
     for step in range(per + stages):
         if step < per:
             first_half(step)
+        if step == 0:
+            search()
         if step == per - 1:
             for j in range(per // 2):
                 contributions(j)
@@ -282,6 +287,22 @@
             reduce_copy(j, b).wait_send()
         wg_copies[j].wait()
     ig_copy.wait()
+
+
+def finish(n_copies, counts, wg_in, ig_in, wg_out, ig_out, sems):
+    per = wg_in.shape[0]
+    rows = ig_in.shape[0] // n_copies
+    copies = []
+    for i in range(n_copies):
+        part = pl.ds(i * rows, rows)
+        copy = pltpu.make_async_copy(ig_in.at[part], ig_out.at[part], sems.at[i])
+        copy.start()
+        copies.append(copy)
+    first = lax.axis_index("dp") * per
+    for j in range(per):
+        wg_out[j] = jnp.where(first + j < counts[0], wg_in[j], 0.0)
+    for copy in copies:
+        copy.wait()
 
 
 def shards(n_t, n_dp, hidden, out_grad, weights, block_rows, block_cols, counts):
@@ -340,8 +361,19 @@
         ),
         cost_estimate=pl.CostEstimate(flops=flops, bytes_accessed=6 * 2**20, transcendentals=0),
     )(counts, block_rows, block_cols, hidden, out_grad, w)
-    live = lax.axis_index("dp") * per + jnp.arange(per, dtype=jnp.int32) < counts[0]
-    return jnp.where(live[:, None, None], wg, 0.0)[None], ig
+    n_copies = math.gcd(tokens // 16, 12)
+    vmem = pl.BlockSpec(memory_space=pltpu.VMEM)
+    wg, ig = pl.pallas_call(
+        functools.partial(finish, n_copies),
+        out_shape=(
+            jax.ShapeDtypeStruct((per, blk, blk), jnp.float32),
+            jax.ShapeDtypeStruct((tokens, width), jnp.bfloat16),
+        ),
+        in_specs=[pl.BlockSpec(memory_space=pltpu.SMEM), vmem, hbm],
+        out_specs=(vmem, hbm),
+        scratch_shapes=[pltpu.SemaphoreType.DMA((n_copies,))],
+    )(counts, wg, ig)
+    return wg[None], ig
 
 
 def solution(mesh):

time: 58.9 us -> 98.7 us (1.68)
  Pallas kernels: 53.1 us -> 97.2 us
  local copies, waits for them, and re-layouts: 2.5 us -> 0 us
  other arithmetic: 1.75 us -> 0 us
    pallas_call x0 -> x1, Pallas kernels: none -> 44.5 us  [shards(): pl.pallas_call(functools.partial(finish, n_copies), out_shape=(jax.ShapeD...]
    unnamed x1 -> x0, local copies, waits for them, and re-layouts: 2.5 us -> none
    broadcast_in_dim x1 -> x0, other arithmetic: 1.74 us -> none  [shards(): return (jnp.where(live[:, None, None], wg, 0.0)[None], ig)]
where the time goes in v3:
time: 98.7 us; the launch traced here: 98.5 us
  Pallas kernels  97.2 us (98%)
  between operations  1.29 us (1%)
    pallas_call x1, Pallas kernels, shards(): pl.pallas_call(functools.partial(kernel, n_t, n_dp, per, panel), out_shap...  52.6 us
    pallas_call x1, Pallas kernels, shards(): pl.pallas_call(functools.partial(finish, n_copies), out_shape=(jax.ShapeD...  44.5 us

profile of v3, /device:TPU:0, one launch (start us, length us, event | category | flops | bytes accessed | tf_op | source)
XLA Modules:
  0.0 98.5 jit_solution(13419913737892734980)
XLA Ops:
  1.3 52.6 %shard_map.77 = (f32[4,128,128]{2,1,0:T(8,128)}, bf16[192,3584]{1,0:T(8,128)(2,1)}) custom-call(s32[1]{0:T(128)S(6)} %copy.8.counts, s32[1,32]{1,0:T(1,128)} %rows_ref.1, s32[1,32]{1,0:T(1,128)} %cols_ref.1, bf16[192,3584]{1,0:T(8,128)(2,1)} %hid_hbm.1, bf16[48,8192]{1,0:T(8,128)(2,1)} %og_hbm.1, bf16[32,128,128]{2,1,0:T(8,128)(2,1)} %bitcast.2), custom_call_target="tpu_custom_call" | custom-call | flops 402653184 | bytes 6291456 | tf_op jit(solution)/shard_map/pallas_call | solution.py:319
  53.9 44.5 %shard_map.78 = (f32[4,128,128]{2,1,0:T(8,128)}, bf16[192,3584]{1,0:T(8,128)(2,1)}) custom-call(s32[1]{0:T(128)S(6)} %copy.8.counts, f32[4,128,128]{2,1,0:T(8,128)} %get-tuple-element.6.wg_in, bf16[192,3584]{1,0:T(8,128)(2,1)} %get-tuple-element.7.ig_in), custom_call_target="tpu_custom_call" | custom-call | tf_op jit(solution)/shard_map/pallas_call | solution.py:366

commit v4 on v3

--- a/solution.py
+++ b/solution.py
@@ -289,20 +289,12 @@
     ig_copy.wait()
 
 
-def finish(n_copies, counts, wg_in, ig_in, wg_out, ig_out, sems):
+def finish(counts, wg_in, ig_in, wg_out, ig_out):
     per = wg_in.shape[0]
-    rows = ig_in.shape[0] // n_copies
-    copies = []
-    for i in range(n_copies):
-        part = pl.ds(i * rows, rows)
-        copy = pltpu.make_async_copy(ig_in.at[part], ig_out.at[part], sems.at[i])
-        copy.start()
-        copies.append(copy)
     first = lax.axis_index("dp") * per
     for j in range(per):
         wg_out[j] = jnp.where(first + j < counts[0], wg_in[j], 0.0)
-    for copy in copies:
-        copy.wait()
+    ig_out[...] = ig_in[...]
 
 
 def shards(n_t, n_dp, hidden, out_grad, weights, block_rows, block_cols, counts):
@@ -361,17 +353,18 @@
         ),
         cost_estimate=pl.CostEstimate(flops=flops, bytes_accessed=6 * 2**20, transcendentals=0),
     )(counts, block_rows, block_cols, hidden, out_grad, w)
-    n_copies = math.gcd(tokens // 16, 12)
-    vmem = pl.BlockSpec(memory_space=pltpu.VMEM)
+    steps = math.gcd(tokens // 16, 4)
+    whole = pl.BlockSpec((per, blk, blk), lambda i: (0, 0, 0))
+    some = pl.BlockSpec((tokens // steps, width), lambda i: (i, 0))
     wg, ig = pl.pallas_call(
-        functools.partial(finish, n_copies),
+        finish,
+        grid=(steps,),
         out_shape=(
             jax.ShapeDtypeStruct((per, blk, blk), jnp.float32),
             jax.ShapeDtypeStruct((tokens, width), jnp.bfloat16),
         ),
-        in_specs=[pl.BlockSpec(memory_space=pltpu.SMEM), vmem, hbm],
-        out_specs=(vmem, hbm),
-        scratch_shapes=[pltpu.SemaphoreType.DMA((n_copies,))],
+        in_specs=[pl.BlockSpec(memory_space=pltpu.SMEM), whole, some],
+        out_specs=(whole, some),
     )(counts, wg, ig)
     return wg[None], ig
 

time: 98.7 us -> 57.8 us (0.59)
  Pallas kernels: 97.2 us -> 56.3 us
    pallas_call x1, Pallas kernels: 44.5 us -> 3.7 us  [shards(): pl.pallas_call(finish, grid=(steps,), out_shape=(jax.ShapeDtypeStruct((pe...]
where the time goes in v4:
time: 57.8 us; the launch traced here: 57.6 us
  Pallas kernels  56.3 us (97%)
  between operations  1.29 us (2%)
    pallas_call x1, Pallas kernels, shards(): pl.pallas_call(functools.partial(kernel, n_t, n_dp, per, panel), out_shap...  52.6 us
    pallas_call x1, Pallas kernels, shards(): pl.pallas_call(finish, grid=(steps,), out_shape=(jax.ShapeDtypeStruct((pe...  3.7 us

profile of v4, /device:TPU:0, one launch (start us, length us, event | category | flops | bytes accessed | tf_op | source)
XLA Modules:
  0.0 57.6 jit_solution(10203891342455844649)
XLA Ops:
  1.3 52.6 %shard_map.77 = (f32[4,128,128]{2,1,0:T(8,128)}, bf16[192,3584]{1,0:T(8,128)(2,1)}) custom-call(s32[1]{0:T(128)S(6)} %copy.8.counts, s32[1,32]{1,0:T(1,128)} %rows_ref.1, s32[1,32]{1,0:T(1,128)} %cols_ref.1, bf16[192,3584]{1,0:T(8,128)(2,1)} %hid_hbm.1, bf16[48,8192]{1,0:T(8,128)(2,1)} %og_hbm.1, bf16[32,128,128]{2,1,0:T(8,128)(2,1)} %bitcast.2), custom_call_target="tpu_custom_call" | custom-call | flops 402653184 | bytes 6291456 | tf_op jit(solution)/shard_map/pallas_call | solution.py:311
  53.9 3.7 %shard_map.78 = (f32[4,128,128]{2,1,0:T(8,128)}, bf16[192,3584]{1,0:T(8,128)(2,1)}) custom-call(s32[1]{0:T(128)S(6)} %copy.8.counts, f32[4,128,128]{2,1,0:T(8,128)} %get-tuple-element.6.wg_in, bf16[192,3584]{1,0:T(8,128)(2,1)} %get-tuple-element.7.ig_in), custom_call_target="tpu_custom_call" | custom-call | tf_op jit(solution)/shard_map/pallas_call | solution.py:359
